TPU v7x, 32 devices: a whole 2x2x4 slice. The times are simulated.
32 devices in a mesh: slide: 2 (over x), gr: 4 (over y, core), gc: 4 (over z).
Axes of the slice: x: 2, y: 2, z: 4, core: 2. Of those that a mesh axis runs over, the one named last changes fastest.
Arguments:
- features: bfloat16 [128, 32, 512], P(('slide', 'gr'), 'gc'), parts along dimension 0, may hold values from -6 to 6
- out_grad: bfloat16 [128, 32, 512], P(('slide', 'gr'), 'gc'), parts along dimension 0, may hold values from -6 to 6
- w_in: bfloat16 [512, 1024], replicated, may hold values from -0.25 to 0.25
- w_out: bfloat16 [1024, 512], replicated, may hold values from -0.1875 to 0.1875
- decay_row: bfloat16 [128, 32, 1024], P(('slide', 'gr'), 'gc'), parts along dimension 0, may hold values from 0 to 1, as said below
- decay_col: bfloat16 [128, 32, 1024], P(('slide', 'gr'), 'gc'), parts along dimension 0, may hold values from 0 to 1, as said below
- b_proj: float32 [128, 32, 16], P(('slide', 'gr'), 'gc'), parts along dimension 0, may hold values from -6 to 6
- c_proj: float32 [128, 32, 16], P(('slide', 'gr'), 'gc'), parts along dimension 0, may hold values from -6 to 6
- tissue: int32 [128, 32], P(('slide', 'gr'), 'gc'), parts along dimension 0, may hold values from 0 to 1, as said below
Outputs:
- feat_grad: bfloat16 [128, 32, 512], P(('slide', 'gr'), 'gc'), parts along dimension 0
- w_in_grad: float32 [1024, 1024], P('slide'), parts along dimension 0
- w_out_grad: float32 [2048, 512], P('slide'), parts along dimension 0
- decay_row_grad: float32 [128, 32, 1024], P(('slide', 'gr'), 'gc'), parts along dimension 0
- decay_col_grad: float32 [128, 32, 1024], P(('slide', 'gr'), 'gc'), parts along dimension 0
- b_grad: float32 [128, 32, 16], P(('slide', 'gr'), 'gc'), parts along dimension 0
- c_grad: float32 [128, 32, 16], P(('slide', 'gr'), 'gc'), parts along dimension 0
There are 2 independent parts, one for each index of `slide`. A program takes and returns all parts, laid end to end along the dimension named above; an argument that names none is the same for every part. Nothing has to cross between parts.
Inputs may be any that keep to these rules, and one draw needn't show every extreme that they name: 1 marks a tissue tile, 0 background; the share of tissue differs from region to region of the grid. `decay_row`: decays lie in (0, 1], most close to one. `decay_col`: decays lie in (0, 1], most close to one.
All inputs are finite; a program needn't handle non-finite values.
Results may differ from a plain program's by a relative error of at most 0.011.
Values sent between devices are 32-bit elements; how exact they have to be, the bound alone decides.
A program may use at most 128 MiB of HBM per device.

v0:
```python
import math
import jax
import jax.numpy as jnp
from jax import lax
from jax.sharding import PartitionSpec as P


def prefix(part, axis, combine, identity, reverse):
    count = lax.axis_size(axis)
    place = lax.axis_index(axis)
    ahead = count - 1 - place if reverse else place
    gathered = jax.tree.map(lambda a: lax.all_gather(a, axis), part)
    state = jax.tree.map(lambda a, e: jnp.zeros_like(a) + jnp.asarray(e, a.dtype), part, identity)

    def one(turn, state):
        source = count - 1 - turn if reverse else turn
        return combine(
            state, jax.tree.map(lambda a: lax.dynamic_index_in_dim(a, source, 0, False), gathered)
        )

    return lax.fori_loop(0, ahead, one, state)


def chain_pair(earlier, later):
    return (earlier[0] * later[0], later[0][:, None, :] * earlier[1] + later[1])


def chain_identity(totals):
    return (jnp.ones_like(totals[0]), jnp.zeros_like(totals[1]))


def row_entering(totals):
    return prefix(totals, "gc", chain_pair, chain_identity(totals), False)[1]


def row_leaving(totals):
    return prefix(totals, "gc", chain_pair, chain_identity(totals), True)[1]


def block_pass(signal_blk, upstream_blk, row_decay, col_decay, b_proj, c_proj, norm_scale):
    row_count, col_count, inner = signal_blk.shape
    states_n = b_proj.shape[2]
    decay_cols = jnp.moveaxis(row_decay, 1, 0)
    signal_cols = jnp.moveaxis(signal_blk, 1, 0)
    b_cols = jnp.moveaxis(b_proj, 1, 0)

    def row_total_step(carry, inputs):
        product, state = carry
        decay_now, signal_now, b_now = inputs
        source_now = norm_scale * b_now[:, :, None] * signal_now[:, None, :]
        return ((product * decay_now, decay_now[:, None, :] * state + source_now), None)

    start_row = (
        jnp.ones((row_count, inner), jnp.float32),
        jnp.zeros((row_count, states_n, inner), jnp.float32),
    )
    row_totals, unused_row = lax.scan(row_total_step, start_row, (decay_cols, signal_cols, b_cols))
    row_in = row_entering(row_totals)

    def row_emit_step(state, inputs):
        decay_now, signal_now, b_now = inputs
        updated = (
            decay_now[:, None, :] * state + norm_scale * b_now[:, :, None] * signal_now[:, None, :]
        )
        return (updated, updated)

    unused_last, row_state_cols = lax.scan(row_emit_step, row_in, (decay_cols, signal_cols, b_cols))
    row_state = jnp.moveaxis(row_state_cols, 0, 1)

    def col_total_step(carry, inputs):
        product, state = carry
        decay_now, row_now = inputs
        return ((product * decay_now, decay_now[:, None, :] * state + row_now), None)

    start_col = (
        jnp.ones((col_count, inner), jnp.float32),
        jnp.zeros((col_count, states_n, inner), jnp.float32),
    )
    col_totals, unused_col = lax.scan(col_total_step, start_col, (col_decay, row_state))
    col_in = prefix(col_totals, "gr", chain_pair, chain_identity(col_totals), False)[1]

    def col_emit_step(state, inputs):
        decay_now, row_now, c_now, up_now = inputs
        updated = decay_now[:, None, :] * state + row_now
        mixed_now = jnp.sum(c_now[:, :, None] * updated, axis=1)
        c_now_grad = jnp.sum(up_now[:, None, :] * updated, axis=2)
        return (updated, (updated, mixed_now, c_now_grad))

    unused_top, col_outputs = lax.scan(
        col_emit_step, col_in, (col_decay, row_state, c_proj, upstream_blk)
    )
    col_state, mixed, c_part = col_outputs
    col_prev = jnp.concatenate([col_in[None], col_state[:-1]], axis=0)
    col_next = jnp.concatenate([col_decay[1:], jnp.ones_like(col_decay[:1])], axis=0)

    def col_back_total(carry, inputs):
        product, adjoint = carry
        next_now, c_now, up_now = inputs
        injected = c_now[:, :, None] * up_now[:, None, :]
        return ((product * next_now, next_now[:, None, :] * adjoint + injected), None)

    back_totals, unused_back = lax.scan(
        col_back_total, start_col, (col_next, c_proj, upstream_blk), reverse=True
    )
    col_out = (col_decay[0] * back_totals[0], col_decay[0][:, None, :] * back_totals[1])
    col_back = prefix(col_out, "gr", chain_pair, chain_identity(col_out), True)[1]

    def col_back_emit(adjoint, inputs):
        next_now, c_now, up_now, prev_now = inputs
        updated = next_now[:, None, :] * adjoint + c_now[:, :, None] * up_now[:, None, :]
        return (updated, (updated, jnp.sum(updated * prev_now, axis=1)))

    unused_first, back_outputs = lax.scan(
        col_back_emit, col_back, (col_next, c_proj, upstream_blk, col_prev), reverse=True
    )
    col_adj, col_dgrad = back_outputs
    row_next = jnp.concatenate([decay_cols[1:], jnp.ones_like(decay_cols[:1])], axis=0)
    col_adj_cols = jnp.moveaxis(col_adj, 1, 0)
    row_prev_cols = jnp.concatenate([row_in[None], row_state_cols[:-1]], axis=0)

    def row_back_total(carry, inputs):
        product, adjoint = carry
        next_now, adj_now = inputs
        return ((product * next_now, next_now[:, None, :] * adjoint + adj_now), None)

    row_back_totals, unused_rb = lax.scan(
        row_back_total, start_row, (row_next, col_adj_cols), reverse=True
    )
    row_back = row_leaving(
        (decay_cols[0] * row_back_totals[0], decay_cols[0][:, None, :] * row_back_totals[1])
    )

    def row_back_emit(adjoint, inputs):
        next_now, adj_now, prev_now, signal_now, b_now = inputs
        updated = next_now[:, None, :] * adjoint + adj_now
        dgrad_now = jnp.sum(updated * prev_now, axis=1)
        signal_now_part = norm_scale * jnp.sum(b_now[:, :, None] * updated, axis=1)
        b_now_part = norm_scale * jnp.sum(signal_now[:, None, :] * updated, axis=2)
        return (updated, (dgrad_now, signal_now_part, b_now_part))

    unused_rf, row_outputs = lax.scan(
        row_back_emit,
        row_back,
        (row_next, col_adj_cols, row_prev_cols, signal_cols, b_cols),
        reverse=True,
    )
    row_dgrad = jnp.moveaxis(row_outputs[0], 0, 1)
    signal_part = jnp.moveaxis(row_outputs[1], 0, 1)
    b_part = jnp.moveaxis(row_outputs[2], 0, 1)
    return (mixed, signal_part, row_dgrad, col_dgrad, b_part, c_part)


def shards(features, out_grad, w_in, w_out, decay_row, decay_col, b_proj, c_proj, tissue):
    row_count, col_count, model_width = features.shape
    inner = w_in.shape[1]
    grid_cells = row_count * lax.axis_size("gr") * col_count * lax.axis_size("gc")
    norm_scale = 1.0 / math.sqrt(grid_cells)
    feat_rows = features.reshape(row_count * col_count, model_width)
    grad_rows = out_grad.reshape(row_count * col_count, model_width)
    tissue_keep = tissue.astype(jnp.float32)[:, :, None]
    projected = jnp.dot(feat_rows, w_in, preferred_element_type=jnp.float32).reshape(
        row_count, col_count, inner
    )
    signal = (tissue_keep * projected).astype(jnp.bfloat16)
    upstream = lax.dot_general(
        grad_rows, w_out, (((1,), (1,)), ((), ())), preferred_element_type=jnp.float32
    )
    upstream = upstream.reshape(row_count, col_count, inner).astype(jnp.bfloat16)
    mixed_parts, signal_parts, row_parts, col_parts = ([], [], [], [])
    b_grad = jnp.zeros(b_proj.shape, jnp.float32)
    c_grad = jnp.zeros(c_proj.shape, jnp.float32)
    outcome = block_pass(
        signal.astype(jnp.float32),
        upstream.astype(jnp.float32),
        decay_row.astype(jnp.float32),
        decay_col.astype(jnp.float32),
        b_proj,
        c_proj,
        norm_scale,
    )
    mixed_parts.append(outcome[0])
    signal_parts.append(outcome[1])
    row_parts.append(outcome[2])
    col_parts.append(outcome[3])
    b_grad = b_grad + outcome[4]
    c_grad = c_grad + outcome[5]
    mixed = mixed_parts[0].astype(jnp.bfloat16)
    signal_grad = (tissue_keep * signal_parts[0]).astype(jnp.bfloat16)
    grad_flat = signal_grad.reshape(row_count * col_count, inner)
    feat_grad = lax.dot_general(
        grad_flat, w_in, (((1,), (1,)), ((), ())), preferred_element_type=jnp.float32
    )
    feat_grad = feat_grad.astype(jnp.bfloat16).reshape(row_count, col_count, model_width)
    w_in_local = lax.dot_general(
        feat_rows, grad_flat, (((0,), (0,)), ((), ())), preferred_element_type=jnp.float32
    )
    mixed_flat = mixed.reshape(row_count * col_count, inner)
    w_out_local = lax.dot_general(
        mixed_flat, grad_rows, (((0,), (0,)), ((), ())), preferred_element_type=jnp.float32
    )
    w_in_grad, w_out_grad = lax.psum((w_in_local, w_out_local), ("gr", "gc"))
    decay_row_grad = row_parts[0]
    decay_col_grad = col_parts[0]
    return (feat_grad, w_in_grad, w_out_grad, decay_row_grad, decay_col_grad, b_grad, c_grad)


def solution(mesh):
    in_specs = (
        P(("slide", "gr"), "gc", None),
        P(("slide", "gr"), "gc", None),
        P(),
        P(),
        P(("slide", "gr"), "gc", None),
        P(("slide", "gr"), "gc", None),
        P(("slide", "gr"), "gc", None),
        P(("slide", "gr"), "gc", None),
        P(("slide", "gr"), "gc"),
    )
    out_specs = (
        P(("slide", "gr"), "gc", None),
        P("slide", None),
        P("slide", None),
        P(("slide", "gr"), "gc", None),
        P(("slide", "gr"), "gc", None),
        P(("slide", "gr"), "gc", None),
        P(("slide", "gr"), "gc", None),
    )
    return jax.shard_map(shards, mesh=mesh, in_specs=in_specs, out_specs=out_specs, check_vma=False)
```

profile of v0, /device:TPU:0, one launch (start us, length us, event | category | flops | bytes accessed | tf_op | source)
XLA Modules:
  0.0 639.7 jit_solution(3221062963915205826)
XLA Ops:
  11.6 3.2 while.187
  21.0 37.7 %while.186 = (s32[]{:T(128)}, f32[8,1024]{1,0:T(8,128)S(1)}, f32[8,16,1024]{2,1,0:T(8,128)S(1)}, f32[16,8,1024]{2,1,0:T(8,128)}, f32[16,8,16]{2,1,0:T(8,128)}, /...) while((s32[]{:T(128)}, f32[8,1024]{1,0:T(8,128)S(1)}, ...), condition=%wide.region_1.2_spmd.clone, body=%wide.region_0.1_spmd.clone.sunk | while | flops 540676 | bytes 1312384 | solution.py:102
  59.7 18.5 %all-gather.2 = f32[64,1024]{1,0:T(8,128)S(1)} all-gather(f32[16,1024]{1,0:T(8,128)S(1)} %get-tuple-element.996), channel_id=4, replica_groups=mesh['slide'=2,'gr'=4,'gc'=4] {'gc'}, dimensions={0}, use_global_device_ids=true | all-gather | bytes 327680 | tf_op jit(solution)/shard_map/all_gather | solution.py:12
  78.2 25.4 %all-gather.15.cloned.1.call-done = f32[64,16,1024]{2,1,0:T(8,128)} async-done(((f32[16,16,1024]{2,1,0:T(8,128)}), f32[64,16,1024]{2,1,0:T(8,128)}) %all-gather.15.cloned.1.call-update) | async-done | bytes 4194320 | tf_op jit(solution)/shard_map/all_gather | solution.py:12
  103.8 22.9 %while.180 = (s32[]{:T(128)}, f32[16,16,1024]{2,1,0:T(8,128)S(1)}, f32[8,16,16,1024]{3,2,1,0:T(8,128)}, f32[8,16,1024]{2,1,0:T(8,128)}, f32[8,16,16]{2,1,0:T(8,128)}, /*index=5*/f32[8,16,1024]{2,1,0:T(8,128)}, s32[]{:T(128)}) while((s32[]{:T(128)}, f32[16,16,1024]{2,1,0:T(8,128)S(1)}, f32[8,16,16,1024]{3,2,1,0:T(8,128)}, ...), condition=%wide.region_9.10_spmd, body=%wide.region_8.9_spmd.sunk | while | flops 786690 | bytes 3542613 | solution.py:67
  126.7 8.4 %copy.71 = f32[8,16,16,1024]{3,2,0,1:T(8,128)} copy(f32[8,16,16,1024]{3,2,1,0:T(8,128)} %get-tuple-element.999) | data formatting | bytes 16777216 | tf_op jit(solution)/shard_map/while | solution.py:67
  135.1 33.2 %while.188 = (s32[]{:T(128)}, f32[8,1024]{1,0:T(8,128)S(1)}, f32[8,16,1024]{2,1,0:T(8,128)S(1)}, f32[16,8,1024]{2,1,0:T(8,128)}, f32[16,8,16,1024]{3,2,1,0:T(8,128)}, /*index=5*/s32[]{:T(128)}, s32[]{:T(128)}) while((s32[]{:T(128)}, f32[8,1024]{1,0:T(8,128)S(1)}, f32[8,16,1024]{2,1,0:T(8,128)S(1)}, f32[16,8,1024]{2,1,0:T(8,128)}, ...), condition=%wide.region_11.12_spmd.clone, body=%wide.region_10.11_spmd.clone.sunk | while | flops 409603 | bytes 1736800 | solution.py:79
  170.9 5.4 all-gather
  177.1 4.0 while.178
  181.2 6.1 all-gather.4
  187.3 9.1 %all-gather.17.cloned.1.call-done = f32[32,16,1024]{2,1,0:T(8,128)} async-done(((f32[8,16,1024]{2,1,0:T(8,128)}), f32[32,16,1024]{2,1,0:T(8,128)}) %all-gather.17.cloned.1.call-update) | async-done | bytes 2097168 | tf_op jit(solution)/shard_map/all_gather | solution.py:12
  198.3 79.2 %while.182 = (s32[]{:T(128)}, f32[8,16,1024]{2,1,0:T(8,128)S(1)}, f32[16,8,16,1024]{3,2,1,0:T(8,128)}, bf16[16,8,1024]{2,1,0:T(8,128)(2,1)}, f32[16,8,16]{2,1,0:...) while((s32[]{:T(128)}, f32[8,16,1024]{2,1,0:T(8,128)S(1)}, ...), condition=%wide.region_17.18_spmd, body=%wide.region_14.17_spmd.sunk | while | flops 778114 | bytes 2875505 | solution.py:89
  277.4 4.1 slice.24
  281.5 4.1 pad_maximum_fusion
  285.6 4.3 broadcast.84.clone
  290.0 57.4 %while.183 = (s32[]{:T(128)}, f32[8,16,1024]{2,1,0:T(8,128)S(1)}, f32[16,8,16,1024]{3,2,0,1:T(8,128)}, f32[16,8,1024]{2,1,0:T(8,128)S(1)}, f32[16,8,1024]{2,1,0:...) while((s32[]{:T(128)}, f32[8,16,1024]{2,1,0:T(8,128)S(1)}, ...), condition=%wide.region_20.21_spmd, body=%wide.region_18.20_spmd.sunk | while | flops 647171 | bytes 2918021 | solution.py:113
  348.2 29.1 %while.189 = (s32[]{:T(128)}, f32[16,1024]{1,0:T(8,128)S(1)}, f32[16,16,1024]{2,1,0:T(8,128)}, f32[8,16,1024]{2,1,0:T(8,128)}, f32[8,16,16,1024]{3,2,1,0:T(8,128)}, /*index=5*/s32[]{:T(128)}, s32[]{:T(128)}, s32[]{:T(128)}) while((s32[]{:T(128)}, f32[16,1024]{1,0:T(8,128)S(1)}, f32[16,16,1024]{2,1,0:T(8,128)}, ...), condition=%wide.region_22.23_spmd.clone, body=%wide.region_21.22_spmd.clone.sunk | while | flops 819204 | bytes 3473524 | solution.py:126
  379.8 3.8 slice.25
  383.6 4.2 pad_maximum_fusion.1
  388.6 16.8 %all-gather.6 = f32[64,1024]{1,0:T(8,128)S(1)} all-gather(f32[16,1024]{1,0:T(8,128)S(1)} %fusion.17), channel_id=8, replica_groups=mesh['slide'=2,'gr'=4,'gc'=4] {'gc'}, dimensions={0}, use_global_device_ids=true | all-gather | bytes 327680 | tf_op jit(solution)/shard_map/all_gather | solution.py:12
  407.3 60.0 %all-gather.19.cloned.1.call-done = f32[64,16,1024]{2,1,0:T(8,128)} async-done(((f32[16,16,1024]{2,1,0:T(8,128)}), f32[64,16,1024]{2,1,0:T(8,128)}) %all-gather.19.cloned.1.call-update) | async-done | bytes 4194320 | tf_op jit(solution)/shard_map/all_gather | solution.py:12
  467.3 5.5 while.184
  473.0 40.8 %while.185 = (s32[]{:T(128)}, f32[16,16,1024]{2,1,0:T(8,128)S(1)}, f32[8,16,1024]{2,0,1:T(8,128)S(1)}, f32[8,16,1024]{2,0,1:T(8,128)S(1)}, f32[8,16,16]{2,0,1:T(...) while((s32[]{:T(128)}, f32[16,16,1024]{2,1,0:T(8,128)S(1)}, ...), condition=%wide.region_29.30_spmd, body=%wide.region_25.29_spmd.sunk | while | flops 2080771 | bytes 5382305 | solution.py:141
  516.8 110.4 %all-reduce.5.cloned.1.call-done = (f32[512,1024]{0,1:T(8,128)}, f32[1024,512]{1,0:T(8,128)}) async-done(((f32[512,1024]{0,1:T(8,128)}, f32[1024,512]{1,0:T(8,128)}), (f32[512,1024]{0,1:T(8,128)}, f32[1024,512]{1,0:T(8,128)})) %all-reduce.5.cloned.1.call-update) | async-done | bytes 4194320 | tf_op jit(solution)/shard_map/psum | solution.py:201
  (529 shorter events, 342.6 us)
Async XLA Ops:
  7.2 2.0 copy-start
  7.2 96.4 %all-gather.15.cloned.1.call-start = ((), (), s32[]{:S(2)}) async-start(), calls=%async_computation.1 | async-start | bytes 5242880 | tf_op jit(solution)/shard_map/all_gather | solution.py:12
  9.2 6.7 %copy-start.9 = (bf16[16,8,1024]{2,1,0:T(8,128)(2,1)S(1)}, bf16[16,8,1024]{2,1,0:T(8,128)(2,1)}, u32[]{:S(2)}) copy-start(bf16[16,8,1024]{2,1,0:T(8,128)(2,1)} %param.38) | copy-start | bytes 786436
  14.8 1.0 copy-start.1
  14.8 1.9 copy-start.10
  14.9 88.8 %copy-start.6 = (f32[8,16,1024]{2,1,0:T(8,128)}, f32[8,16,1024]{2,1,0:T(8,128)S(1)}, u32[]{:S(2)}) copy-start(f32[8,16,1024]{2,1,0:T(8,128)S(1)} %get-tuple-element.2221) | copy-start | bytes 1572868
  14.9 88.8 %copy-start.8 = (f32[8,16,1024]{2,1,0:T(8,128)}, f32[8,16,1024]{2,1,0:T(8,128)S(1)}, u32[]{:S(2)}) copy-start(f32[8,16,1024]{2,1,0:T(8,128)S(1)} %get-tuple-element.2223) | copy-start | bytes 1572868
  15.8 161.2 %all-gather.13.cloned.1.call-start = ((), (), s32[]{:S(2)}) async-start(), calls=%async_computation | async-start | bytes 2621440 | tf_op jit(solution)/shard_map/all_gather | solution.py:12
  59.6 136.7 %all-gather.17.cloned.1.call-start = ((), (), s32[]{:S(2)}) async-start(), calls=%async_computation.2 | async-start | bytes 2621440 | tf_op jit(solution)/shard_map/all_gather | solution.py:12
  126.7 8.4 %copy-start.4 = (f32[8,16,1024]{2,1,0:T(8,128)S(1)}, f32[8,16,1024]{2,1,0:T(8,128)}, u32[]{:S(2)}) copy-start(f32[8,16,1024]{2,1,0:T(8,128)} %custom-call.5) | copy-start | bytes 1572868
  135.1 34.1 %copy-start.7 = (f32[8,16,1024]{2,1,0:T(8,128)S(1)}, f32[8,16,1024]{2,1,0:T(8,128)}, u32[]{:S(2)}) copy-start(f32[8,16,1024]{2,1,0:T(8,128)} %get-tuple-element.2222) | copy-start | bytes 1572868
  168.3 0.8 copy-start.5
  169.2 298.1 %all-gather.19.cloned.1.call-start = ((), (), s32[]{:S(2)}) async-start(), calls=%async_computation.3 | async-start | bytes 5242880 | tf_op jit(solution)/shard_map/all_gather | solution.py:12
  196.4 0.8 copy-start.2
  277.4 4.1 copy-start.3
  347.4 0.8 copy-start.12
  379.6 247.6 %all-reduce.5.cloned.1.call-start = ((), (), s32[]{:S(2)}) async-start(), calls=%async_computation.4 | async-start | bytes 8388608 | tf_op jit(solution)/shard_map/psum | solution.py:201
  383.6 21.9 %copy-start.13 = (bf16[16,8,1024]{2,1,0:T(8,128)(2,1)S(1)}, bf16[16,8,1024]{2,1,0:T(8,128)(2,1)}, u32[]{:S(2)}) copy-start(bf16[16,8,1024]{2,1,0:T(8,128)(2,1)} %get-tuple-element.1009) | copy-start | bytes 786436
  383.6 21.9 %copy-start.14 = (bf16[16,8,512]{2,1,0:T(8,128)(2,1)S(1)}, bf16[16,8,512]{2,1,0:T(8,128)(2,1)}, u32[]{:S(2)}) copy-start(bf16[16,8,512]{2,1,0:T(8,128)(2,1)} %param.34) | copy-start | bytes 393220
  472.9 40.8 %copy-start.15 = (bf16[16,8,512]{2,1,0:T(8,128)(2,1)S(1)}, bf16[16,8,512]{2,1,0:T(8,128)(2,1)}, u32[]{:S(2)}) copy-start(bf16[16,8,512]{2,1,0:T(8,128)(2,1)} %param.33) | copy-start | bytes 393220
  513.7 1.9 copy-start.11
  513.8 1.9 copy-start.16
Sparse Core Ops, SparseCore 0:
  15.9 87.5 all-gather.14
  105.1 21.1 all-gather.12
  169.3 26.9 all-gather.16
  379.8 87.4 all-gather.18
  515.8 111.3 all-reduce.4
where the time goes:
time: 652 us; the launch traced here: 640 us
  waiting for transfers between devices  205 us (31%)
  other arithmetic  182 us (28%)
  local copies, waits for them, and re-layouts  181 us (28%)
  blocking collectives  46.9 us (7%)
  between operations  14.2 us (2%)
  matrix products  8.64 us (1%)
    psum x1, waiting for transfers between devices, shards(): w_in_grad, w_out_grad = lax.psum((w_in_local, w_out_local), ('gr', 'gc'))  110 us
    all_gather x4, waiting for transfers between devices, prefix(): gathered = jax.tree.map(lambda a: lax.all_gather(a, axis), part)  94.4 us
    all_gather x4, blocking collectives, prefix(): gathered = jax.tree.map(lambda a: lax.all_gather(a, axis), part)  46.9 us
    dynamic_update_slice x80, local copies, waits for them, and re-layouts, block_pass(): lax.scan(col_emit_step, col_in, (col_decay, row_state, c_proj, upstream_b...  46.4 us
    mul x32, local copies, waits for them, and re-layouts, col_back_emit(): c_now[:, :, None] * up_now[:, None, :]  23.5 us
    mul x32, local copies, waits for them, and re-layouts, col_back_total(): injected = c_now[:, :, None] * up_now[:, None, :]  23.2 us
    reduce_sum x16, other arithmetic, col_emit_step(): c_now_grad = jnp.sum(up_now[:, None, :] * updated, axis=2)  22.9 us
    add x8, other arithmetic, row_back_total(): next_now[:, None, :] * adjoint + adj_now  22.2 us
  transfers between devices with their start and end apart: 5, of which 4 were waited for; matrix products, arithmetic and copies ran while one was open for 20% of the time, Pallas kernels for 0%

commit v1 on v0

--- a/solution.py
+++ b/solution.py
@@ -198,7 +198,7 @@
     w_out_local = lax.dot_general(
         mixed_flat, grad_rows, (((0,), (0,)), ((), ())), preferred_element_type=jnp.float32
     )
-    w_in_grad, w_out_grad = lax.psum((w_in_local, w_out_local), ("gr", "gc"))
+    w_in_grad, w_out_grad = lax.psum(lax.psum((w_in_local, w_out_local), "gc"), "gr")
     decay_row_grad = row_parts[0]
     decay_col_grad = col_parts[0]
     return (feat_grad, w_in_grad, w_out_grad, decay_row_grad, decay_col_grad, b_grad, c_grad)

time: 652 us -> 783 us (1.20)
  waiting for transfers between devices: 205 us -> 335 us
    psum x1 -> x2, waiting for transfers between devices: 110 us -> 241 us  [the longest x1 155 us: shards(): lax.psum((w_in_local, w_out_local), 'gc')]
  transfers between devices with their start and end apart: 5 -> 6, of which waited for: 4 -> 5; matrix products, arithmetic and copies ran while one was open for 20% -> 16% of each run, Pallas kernels for 0% -> 0%
where the time goes in v1:
time: 783 us; the launch traced here: 771 us
  waiting for transfers between devices  335 us (43%)
  other arithmetic  182 us (23%)
  local copies, waits for them, and re-layouts  180 us (23%)
  blocking collectives  46.9 us (6%)
  between operations  14.6 us (2%)
  matrix products  8.65 us (1%)
    psum x1, waiting for transfers between devices, shards(): lax.psum((w_in_local, w_out_local), 'gc')  155 us
    all_gather x4, waiting for transfers between devices, prefix(): gathered = jax.tree.map(lambda a: lax.all_gather(a, axis), part)  94.4 us
    psum x1, waiting for transfers between devices, shards(): lax.psum(lax.psum((w_in_local, w_out_local), 'gc'), 'gr')  86 us
    all_gather x4, blocking collectives, prefix(): gathered = jax.tree.map(lambda a: lax.all_gather(a, axis), part)  46.9 us
    dynamic_update_slice x80, local copies, waits for them, and re-layouts, block_pass(): lax.scan(col_emit_step, col_in, (col_decay, row_state, c_proj, upstream_b...  46.2 us
    mul x32, local copies, waits for them, and re-layouts, col_back_emit(): c_now[:, :, None] * up_now[:, None, :]  23.5 us
    mul x32, local copies, waits for them, and re-layouts, col_back_total(): injected = c_now[:, :, None] * up_now[:, None, :]  23.2 us
    reduce_sum x16, other arithmetic, col_emit_step(): c_now_grad = jnp.sum(up_now[:, None, :] * updated, axis=2)  22.9 us
  transfers between devices with their start and end apart: 6, of which 5 were waited for; matrix products, arithmetic and copies ran while one was open for 16% of the time, Pallas kernels for 0%

profile of v1, /device:TPU:0, one launch (start us, length us, event | category | flops | bytes accessed | tf_op | source)
XLA Modules:
  0.0 770.5 jit_solution(11087940449891722671)
XLA Ops:
  21.0 37.7 %while.186 = (s32[]{:T(128)}, f32[8,1024]{1,0:T(8,128)S(1)}, f32[8,16,1024]{2,1,0:T(8,128)S(1)}, f32[16,8,1024]{2,1,0:T(8,128)}, f32[16,8,16]{2,1,0:T(8,128)}, /...) while((s32[]{:T(128)}, f32[8,1024]{1,0:T(8,128)S(1)}, ...), condition=%wide.region_1.2_spmd.clone, body=%wide.region_0.1_spmd.clone.sunk | while | flops 540676 | bytes 1312384 | solution.py:102
  59.6 18.6 %all-gather.2 = f32[64,1024]{1,0:T(8,128)S(1)} all-gather(f32[16,1024]{1,0:T(8,128)S(1)} %get-tuple-element.996), channel_id=4, replica_groups=mesh['slide'=2,'gr'=4,'gc'=4] {'gc'}, dimensions={0}, use_global_device_ids=true | all-gather | bytes 327680 | tf_op jit(solution)/shard_map/all_gather | solution.py:12
  78.2 25.4 %all-gather.15.cloned.1.call-done = f32[64,16,1024]{2,1,0:T(8,128)} async-done(((f32[16,16,1024]{2,1,0:T(8,128)}), f32[64,16,1024]{2,1,0:T(8,128)}) %all-gather.15.cloned.1.call-update) | async-done | bytes 4194320 | tf_op jit(solution)/shard_map/all_gather | solution.py:12
  103.8 23.0 %while.180 = (s32[]{:T(128)}, f32[16,16,1024]{2,1,0:T(8,128)S(1)}, f32[8,16,16,1024]{3,2,1,0:T(8,128)}, f32[8,16,1024]{2,1,0:T(8,128)}, f32[8,16,16]{2,1,0:T(8,128)}, /*index=5*/f32[8,16,1024]{2,1,0:T(8,128)}, s32[]{:T(128)}) while((s32[]{:T(128)}, f32[16,16,1024]{2,1,0:T(8,128)S(1)}, f32[8,16,16,1024]{3,2,1,0:T(8,128)}, ...), condition=%wide.region_9.10_spmd, body=%wide.region_8.9_spmd.sunk | while | flops 786690 | bytes 3542613 | solution.py:67
  126.8 8.4 %copy.71 = f32[8,16,16,1024]{3,2,0,1:T(8,128)} copy(f32[8,16,16,1024]{3,2,1,0:T(8,128)} %get-tuple-element.999) | data formatting | bytes 16777216 | tf_op jit(solution)/shard_map/while | solution.py:67
  135.2 33.2 %while.188 = (s32[]{:T(128)}, f32[8,1024]{1,0:T(8,128)S(1)}, f32[8,16,1024]{2,1,0:T(8,128)S(1)}, f32[16,8,1024]{2,1,0:T(8,128)}, f32[16,8,16,1024]{3,2,1,0:T(8,128)}, /*index=5*/s32[]{:T(128)}, s32[]{:T(128)}) while((s32[]{:T(128)}, f32[8,1024]{1,0:T(8,128)S(1)}, f32[8,16,1024]{2,1,0:T(8,128)S(1)}, f32[16,8,1024]{2,1,0:T(8,128)}, ...), condition=%wide.region_11.12_spmd.clone, body=%wide.region_10.11_spmd.clone.sunk | while | flops 409603 | bytes 1736800 | solution.py:79
  170.9 5.4 all-gather
  177.2 4.0 while.178
  181.2 6.1 all-gather.4
  187.3 9.0 %all-gather.17.cloned.1.call-done = f32[32,16,1024]{2,1,0:T(8,128)} async-done(((f32[8,16,1024]{2,1,0:T(8,128)}), f32[32,16,1024]{2,1,0:T(8,128)}) %all-gather.17.cloned.1.call-update) | async-done | bytes 2097168 | tf_op jit(solution)/shard_map/all_gather | solution.py:12
  198.3 79.2 %while.182 = (s32[]{:T(128)}, f32[8,16,1024]{2,1,0:T(8,128)S(1)}, f32[16,8,16,1024]{3,2,1,0:T(8,128)}, bf16[16,8,1024]{2,1,0:T(8,128)(2,1)}, f32[16,8,16]{2,1,0:...) while((s32[]{:T(128)}, f32[8,16,1024]{2,1,0:T(8,128)S(1)}, ...), condition=%wide.region_17.18_spmd, body=%wide.region_14.17_spmd.sunk | while | flops 778114 | bytes 2875505 | solution.py:89
  277.5 4.1 slice.24
  281.6 4.1 pad_maximum_fusion
  285.7 4.3 broadcast.84.clone
  290.0 57.3 %while.183 = (s32[]{:T(128)}, f32[8,16,1024]{2,1,0:T(8,128)S(1)}, f32[16,8,16,1024]{3,2,0,1:T(8,128)}, f32[16,8,1024]{2,1,0:T(8,128)S(1)}, f32[16,8,1024]{2,1,0:...) while((s32[]{:T(128)}, f32[8,16,1024]{2,1,0:T(8,128)S(1)}, ...), condition=%wide.region_20.21_spmd, body=%wide.region_18.20_spmd.sunk | while | flops 647171 | bytes 2918021 | solution.py:113
  348.1 29.1 %while.189 = (s32[]{:T(128)}, f32[16,1024]{1,0:T(8,128)S(1)}, f32[16,16,1024]{2,1,0:T(8,128)}, f32[8,16,1024]{2,1,0:T(8,128)}, f32[8,16,16,1024]{3,2,1,0:T(8,128)}, /*index=5*/s32[]{:T(128)}, s32[]{:T(128)}, s32[]{:T(128)}) while((s32[]{:T(128)}, f32[16,1024]{1,0:T(8,128)S(1)}, f32[16,16,1024]{2,1,0:T(8,128)}, ...), condition=%wide.region_22.23_spmd.clone, body=%wide.region_21.22_spmd.clone.sunk | while | flops 819204 | bytes 3473524 | solution.py:126
  379.6 3.8 slice.25
  383.5 4.2 pad_maximum_fusion.1
  388.5 16.8 %all-gather.6 = f32[64,1024]{1,0:T(8,128)S(1)} all-gather(f32[16,1024]{1,0:T(8,128)S(1)} %fusion.17), channel_id=8, replica_groups=mesh['slide'=2,'gr'=4,'gc'=4] {'gc'}, dimensions={0}, use_global_device_ids=true | all-gather | bytes 327680 | tf_op jit(solution)/shard_map/all_gather | solution.py:12
  407.1 59.9 %all-gather.19.cloned.1.call-done = f32[64,16,1024]{2,1,0:T(8,128)} async-done(((f32[16,16,1024]{2,1,0:T(8,128)}), f32[64,16,1024]{2,1,0:T(8,128)}) %all-gather.19.cloned.1.call-update) | async-done | bytes 4194320 | tf_op jit(solution)/shard_map/all_gather | solution.py:12
  467.2 5.5 while.184
  472.8 40.8 %while.185 = (s32[]{:T(128)}, f32[16,16,1024]{2,1,0:T(8,128)S(1)}, f32[8,16,1024]{2,0,1:T(8,128)S(1)}, f32[8,16,1024]{2,0,1:T(8,128)S(1)}, f32[8,16,16]{2,0,1:T(...) while((s32[]{:T(128)}, f32[16,16,1024]{2,1,0:T(8,128)S(1)}, ...), condition=%wide.region_29.30_spmd, body=%wide.region_25.29_spmd.sunk | while | flops 2080771 | bytes 5382305 | solution.py:141
  515.6 154.9 %all-reduce.7.cloned.1.call-done = (f32[512,1024]{0,1:T(8,128)}, f32[1024,512]{1,0:T(8,128)}) async-done(((f32[512,1024]{0,1:T(8,128)}, f32[1024,512]{1,0:T(8,128)}), (f32[512,1024]{0,1:T(8,128)}, f32[1024,512]{1,0:T(8,128)})) %all-reduce.7.cloned.1.call-update) | async-done | bytes 4194320 | tf_op jit(solution)/shard_map/psum | solution.py:201
  671.7 86.0 %all-reduce.9.cloned.1.call-done = (f32[512,1024]{0,1:T(8,128)}, f32[1024,512]{1,0:T(8,128)}) async-done(((f32[512,1024]{0,1:T(8,128)}, f32[1024,512]{1,0:T(8,128)}), (f32[512,1024]{0,1:T(8,128)}, f32[1024,512]{1,0:T(8,128)})) %all-reduce.9.cloned.1.call-update) | async-done | bytes 4194320 | tf_op jit(solution)/shard_map/psum | solution.py:201
  (532 shorter events, 345.7 us)
Async XLA Ops:
  7.2 2.0 copy-start
  7.2 96.4 %all-gather.15.cloned.1.call-start = ((), (), s32[]{:S(2)}) async-start(), calls=%async_computation.1 | async-start | bytes 5242880 | tf_op jit(solution)/shard_map/all_gather | solution.py:12
  9.2 6.7 copy-start.9
  14.8 1.0 copy-start.1
  14.8 1.9 copy-start.10
  14.9 88.8 %copy-start.6 = (f32[8,16,1024]{2,1,0:T(8,128)}, f32[8,16,1024]{2,1,0:T(8,128)S(1)}, u32[]{:S(2)}) copy-start(f32[8,16,1024]{2,1,0:T(8,128)S(1)} %get-tuple-element.2227) | copy-start | bytes 1572868
  14.9 88.8 %copy-start.8 = (f32[8,16,1024]{2,1,0:T(8,128)}, f32[8,16,1024]{2,1,0:T(8,128)S(1)}, u32[]{:S(2)}) copy-start(f32[8,16,1024]{2,1,0:T(8,128)S(1)} %get-tuple-element.2229) | copy-start | bytes 1572868
  15.8 161.3 %all-gather.13.cloned.1.call-start = ((), (), s32[]{:S(2)}) async-start(), calls=%async_computation | async-start | bytes 2621440 | tf_op jit(solution)/shard_map/all_gather | solution.py:12
  59.6 136.8 %all-gather.17.cloned.1.call-start = ((), (), s32[]{:S(2)}) async-start(), calls=%async_computation.2 | async-start | bytes 2621440 | tf_op jit(solution)/shard_map/all_gather | solution.py:12
  126.8 8.4 %copy-start.4 = (f32[8,16,1024]{2,1,0:T(8,128)S(1)}, f32[8,16,1024]{2,1,0:T(8,128)}, u32[]{:S(2)}) copy-start(f32[8,16,1024]{2,1,0:T(8,128)} %custom-call.5) | copy-start | bytes 1572868
  135.2 34.1 %copy-start.7 = (f32[8,16,1024]{2,1,0:T(8,128)S(1)}, f32[8,16,1024]{2,1,0:T(8,128)}, u32[]{:S(2)}) copy-start(f32[8,16,1024]{2,1,0:T(8,128)} %get-tuple-element.2228) | copy-start | bytes 1572868
  168.4 0.8 copy-start.5
  169.2 297.9 %all-gather.19.cloned.1.call-start = ((), (), s32[]{:S(2)}) async-start(), calls=%async_computation.3 | async-start | bytes 5242880 | tf_op jit(solution)/shard_map/all_gather | solution.py:12
  196.4 0.9 copy-start.2
  277.5 4.1 copy-start.3
  347.3 0.8 copy-start.12
  379.5 291.0 %all-reduce.7.cloned.1.call-start = ((), (), s32[]{:S(2)}) async-start(), calls=%async_computation.4 | async-start | bytes 8388608 | tf_op jit(solution)/shard_map/psum | solution.py:201
  383.4 21.9 %copy-start.13 = (bf16[16,8,1024]{2,1,0:T(8,128)(2,1)S(1)}, bf16[16,8,1024]{2,1,0:T(8,128)(2,1)}, u32[]{:S(2)}) copy-start(bf16[16,8,1024]{2,1,0:T(8,128)(2,1)} %get-tuple-element.1009) | copy-start | bytes 786436
  383.4 21.9 %copy-start.14 = (bf16[16,8,512]{2,1,0:T(8,128)(2,1)S(1)}, bf16[16,8,512]{2,1,0:T(8,128)(2,1)}, u32[]{:S(2)}) copy-start(bf16[16,8,512]{2,1,0:T(8,128)(2,1)} %param.34) | copy-start | bytes 393220
  472.8 40.8 %copy-start.15 = (bf16[16,8,512]{2,1,0:T(8,128)(2,1)S(1)}, bf16[16,8,512]{2,1,0:T(8,128)(2,1)}, u32[]{:S(2)}) copy-start(bf16[16,8,512]{2,1,0:T(8,128)(2,1)} %param.33) | copy-start | bytes 393220
  513.6 1.9 copy-start.11
  513.6 1.9 copy-start.16
  515.6 242.2 %all-reduce.9.cloned.1.call-start = ((), (), s32[]{:S(2)}) async-start(), calls=%async_computation.5 | async-start | bytes 8388608 | tf_op jit(solution)/shard_map/psum | solution.py:201
Sparse Core Ops, SparseCore 0:
  15.9 87.5 all-gather.14
  105.1 21.1 all-gather.12
  169.3 26.9 all-gather.16
  379.6 87.4 all-gather.18
  515.7 154.8 all-reduce.6
  673.0 84.6 all-reduce.8
